TPU v7x, 32 devices: a whole 2x2x4 slice. The times are simulated.
32 devices in a mesh: dp: 8 (over y, x, core), fsdp: 4 (over z).
Axes of the slice: x: 2, y: 2, z: 4, core: 2. Of those that a mesh axis runs over, the one named last changes fastest.
Arguments:
- latents: bfloat16 [8, 2, 256, 2432], P('dp', None, 'fsdp'), may hold values from -6 to 6
- targets: bfloat16 [8, 2, 256, 2432], P('dp', None, 'fsdp'), may hold values from -6 to 6
- frozen_weight: bfloat16 [2432, 2432], P('fsdp'), may hold values from -0.125 to 0.125
- adapter_down: bfloat16 [7, 64, 2432], P(None, None, 'dp'), may hold values from -0.125 to 0.125
- adapter_up: bfloat16 [7, 64, 2432], P(None, None, 'dp'), may hold values from -0.75 to 0.75
- categories: int32 [8], P('dp'), may hold values from 0 to 6
- timesteps: int32 [8], P('dp'), may hold values from 0 to 999
Outputs:
- grad_down: float32 [7, 64, 2432], P(None, None, 'dp')
- grad_up: float32 [7, 64, 2432], P(None, None, 'dp')
- losses: float32 [8], P('dp')
All inputs are finite; a program needn't handle non-finite values.
Results may differ from a plain program's by a relative error of at most 0.0048.
Values may be sent and summed in bfloat16 or wider, within the bound.
A program may use at most 128 MiB of HBM per device.

v0:
```python
import jax
import jax.numpy as jnp
from jax import lax
from jax.sharding import PartitionSpec as P

ADAPTER_SCALE = 0.5
BETA = 1.0
LOSS_SCALE = 64.0


def local(latents, targets, frozen_weight, adapter_down, adapter_up, categories, timesteps):
    pair_local, _, row_local, feat_width = latents.shape
    class_total = adapter_down.shape[0]
    adapter_rank_width = adapter_down.shape[1]
    sample_rows = row_local * lax.axis_size("fsdp")
    flat_in = latents.reshape(pair_local * 2 * row_local, feat_width)
    down_full, up_full = (
        lax.all_gather(adapter_down, "dp", axis=2, tiled=True),
        lax.all_gather(adapter_up, "dp", axis=2, tiled=True),
    )
    base_out = jnp.dot(
        flat_in,
        lax.all_gather(frozen_weight, "fsdp", axis=0, tiled=True),
        preferred_element_type=jnp.float32,
    )
    selected_down = jnp.take(down_full, categories, axis=0)
    selected_up = jnp.take(up_full, categories, axis=0)
    grouped = latents.reshape(pair_local, 2 * row_local, feat_width)
    hidden_state = jnp.einsum(
        "psd,prd->psr", grouped, selected_down, preferred_element_type=jnp.float32
    ).astype(jnp.bfloat16)
    weight_change = ADAPTER_SCALE * jnp.einsum(
        "psr,prd->psd", hidden_state, selected_up, preferred_element_type=jnp.float32
    )
    weight_change = weight_change.reshape(pair_local, 2, row_local, feat_width)
    resid = base_out.reshape(pair_local, 2, row_local, feat_width) - targets.astype(jnp.float32)
    partial_err = jnp.sum(weight_change * (2.0 * resid + weight_change), axis=(2, 3))
    onehot = (categories[:, None] == jnp.arange(class_total, dtype=jnp.int32)[None, :]).astype(
        jnp.float32
    )
    errdiff = lax.psum(partial_err, "fsdp") / sample_rows
    counts = lax.psum(jnp.sum(onehot, axis=0), "dp")
    kappa = BETA * (0.5 + timesteps.astype(jnp.float32) / 1000.0)
    zvalue = kappa * (errdiff[:, 0] - errdiff[:, 1])
    losses = jax.nn.softplus(zvalue)
    pair_total = jnp.sum(onehot * counts[None, :], axis=1)
    coef_pair = LOSS_SCALE * kappa * jax.nn.sigmoid(zvalue) / pair_total
    signs = jnp.array([2.0, -2.0], dtype=jnp.float32)
    coefficient = coef_pair[:, None] * signs[None, :] / sample_rows
    update = (resid + weight_change).astype(jnp.bfloat16)
    hidden_k = hidden_state.reshape(pair_local, 2, row_local, adapter_rank_width)
    up_gradient_k = jnp.einsum(
        "pktr,pktd->pkrd", hidden_k, update, preferred_element_type=jnp.float32
    )
    back = jnp.einsum(
        "pktd,prd->pktr", update, selected_up, preferred_element_type=jnp.float32
    ).astype(jnp.bfloat16)
    down_gradient_k = jnp.einsum(
        "pktr,pktd->pkrd", back, latents, preferred_element_type=jnp.float32
    )
    pairwise_up = ADAPTER_SCALE * jnp.sum(coefficient[:, :, None, None] * up_gradient_k, axis=1)
    pairwise_down = ADAPTER_SCALE * jnp.sum(coefficient[:, :, None, None] * down_gradient_k, axis=1)
    pairwise_down, pairwise_up = lax.psum((pairwise_down, pairwise_up), "fsdp")
    dense_down = jnp.einsum("pc,prd->crd", onehot, pairwise_down, precision=lax.Precision.HIGHEST)
    dense_up = jnp.einsum("pc,prd->crd", onehot, pairwise_up, precision=lax.Precision.HIGHEST)
    grad_down, grad_up = (
        lax.psum_scatter(dense_down, "dp", scatter_dimension=2, tiled=True),
        lax.psum_scatter(dense_up, "dp", scatter_dimension=2, tiled=True),
    )
    return (grad_down, grad_up, losses)


def solution(mesh):
    placed = (
        P("dp", None, "fsdp", None),
        P("dp", None, "fsdp", None),
        P("fsdp", None),
        P(None, None, "dp"),
        P(None, None, "dp"),
        P("dp"),
        P("dp"),
    )
    return jax.shard_map(
        local,
        mesh=mesh,
        in_specs=placed,
        out_specs=(P(None, None, "dp"), P(None, None, "dp"), P("dp")),
        check_vma=False,
    )
```

profile of v0, /device:TPU:0, one launch (start us, length us, event | category | flops | bytes accessed | tf_op | source)
XLA Modules:
  0.0 528.0 jit_solution(15645915196502282978)
XLA Ops:
  7.2 2.3 copy.15
  9.6 1.2 copy.17
  10.8 0.7 all-gather.8.cloned.1.call-update
  12.2 15.3 %psum.29 = f32[7]{0:T(128)S(1)} all-reduce(f32[7]{0:T(128)S(1)} %compare_convert_fusion.1), channel_id=1, replica_groups=mesh['dp'=8,'fsdp'=4] {'dp'}, use_global_device_ids=true, to_apply=%region_2.4 | all-reduce | flops 7 | bytes 56 | tf_op jit(solution)/shard_map/psum | solution.py:42
  28.2 0.7 fusion.25
  28.9 24.4 %all-gather.4.cloned.1.call-done = bf16[7,64,2432]{1,0,2:T(8,128)(2,1)} async-done(((bf16[7,64,304]{1,0,2:T(8,128)(2,1)}), bf16[7,64,2432]{1,0,2:T(8,128)(2,1)}) %all-gather.4.cloned.1.call-update) | async-done | bytes 2179088 | tf_op jit(solution)/shard_map/all_gather | solution.py:18
  53.3 3.8 constant_dynamic-slice_fusion.1
  57.1 1.2 copy.26
  58.3 0.3 convolution_convert_fusion.1
  58.7 37.1 %all-gather.6.cloned.1.call-done = bf16[7,64,2432]{1,0,2:T(8,128)(2,1)} async-done(((bf16[7,64,304]{1,0,2:T(8,128)(2,1)}), bf16[7,64,2432]{1,0,2:T(8,128)(2,1)}) %all-gather.6.cloned.1.call-update) | async-done | bytes 2179088 | tf_op jit(solution)/shard_map/all_gather | solution.py:19
  95.8 3.8 constant_dynamic-slice_fusion
  99.6 1.2 copy.27
  100.8 0.3 convolution_multiply_fusion.2
  101.1 202.1 %all-gather.8.cloned.1.call-done = bf16[2432,2432]{1,0:T(8,128)(2,1)} async-done(((bf16[608,2432]{1,0:T(8,128)(2,1)}), bf16[2432,2432]{1,0:T(8,128)(2,1)}) %all-gather.8.cloned.1.call-update) | async-done | bytes 11829264 | tf_op jit(solution)/shard_map/all_gather | solution.py:23
  303.3 6.5 %fusion.10 = (f32[2]{0:T(128)S(1)}, bf16[2,64,2432]{2,1,0:T(8,128)(2,1)S(1)}) fusion(f32[1,2,64,2432]{3,2,1,0:T(8,128)S(1)} %bitcast.65, f32[128,2432]{1,0:T(8,128)S(1)} %convolution_multiply_fusion.2, bf16[1,2,64,2432]{3,2,1,0:T(8,128)(2,1)S(1)} %copy-done.2, bf16[2432,2432]{1,0:T(8,128)(2,1)} %all-gather.8.cloned.1.call-done, ...), kind=kOutput, calls=%fused_computation.12 | convolution fusion | flops 1516634112 | bytes 16187400 | tf_op jit(solution)/shard_map/dot_general | solution.py:21
  309.7 8.6 %psum.28 = f32[1,2]{1,0:T(1,128)S(1)} all-reduce(f32[1,2]{1,0:T(1,128)S(1)} %bitcast.69), channel_id=1, replica_groups=mesh['dp'=8,'fsdp'=4] {'fsdp'}, use_global_device_ids=true, to_apply=%region_1.3 | all-reduce | flops 2 | bytes 16 | tf_op jit(solution)/shard_map/psum | solution.py:41
  318.4 0.6 fusion.31
  321.1 0.9 fusion.8
  322.0 0.3 fusion.9
  322.3 1.1 broadcast_multiply_fusion.2
  323.5 57.7 %all-reduce.3.cloned.1.call-done = (f32[64,2432]{1,0:T(8,128)}, f32[64,2432]{1,0:T(8,128)}) async-done(((f32[64,2432]{1,0:T(8,128)}, f32[64,2432]{1,0:T(8,128)}), (f32[64,2432]{1,0:T(8,128)}, f32[64,2432]{1,0:T(8,128)})) %all-reduce.3.cloned.1.call-update) | async-done | bytes 1245200 | tf_op jit(solution)/shard_map/psum | solution.py:63
  381.2 5.6 %broadcast_multiply_fusion = (f32[7,64,2432]{2,1,0:T(8,128)}, f32[7,64,2432]{2,1,0:T(8,128)}) fusion(f32[64,2432]{1,0:T(8,128)} %get-tuple-element.16, f32[7]{0:T(128)S(1)} %fusion.26, f32[64,2432]{1,0:T(8,128)} %get-tuple-element.15), kind=kLoop, calls=%fused_computation.7 | loop fusion | flops 2179072 | bytes 9961500 | tf_op jit(solution)/shard_map/pc,prd->crd/dot_general | solution.py:65
  386.8 7.9 %copy.24 = f32[7,64,2432]{1,0,2:T(8,128)} copy(f32[7,64,2432]{2,1,0:T(8,128)} %get-tuple-element.19) | data formatting | bytes 8716288
  394.7 9.2 %reshape.196 = f32[2432,448]{1,0:T(8,128)} reshape(f32[2432,7,64]{2,1,0:T(8,128)} %bitcast.63) | data formatting | bytes 8716288
  403.9 7.9 %copy.22 = f32[7,64,2432]{1,0,2:T(8,128)} copy(f32[7,64,2432]{2,1,0:T(8,128)} %get-tuple-element.20) | data formatting | bytes 8716288
  411.8 9.7 %reshape.194 = f32[2432,448]{1,0:T(8,128)} reshape(f32[2432,7,64]{2,1,0:T(8,128)} %bitcast.64) | data formatting | bytes 8716288
  421.7 37.1 %reduce-scatter.9.cloned.1.call-done = f32[304,448]{1,0:T(8,128)} async-done(((f32[2432,448]{1,0:T(8,128)}), f32[304,448]{1,0:T(8,128)}) %reduce-scatter.9.cloned.1.call-update) | async-done | bytes 544784
  458.8 1.4 reshape.197
  460.2 1.3 copy.25
  461.5 55.9 %reduce-scatter.7.cloned.1.call-done = f32[304,448]{1,0:T(8,128)} async-done(((f32[2432,448]{1,0:T(8,128)}), f32[304,448]{1,0:T(8,128)}) %reduce-scatter.7.cloned.1.call-update) | async-done | bytes 544784
  517.3 1.4 reshape.195
  518.8 1.3 copy.23
  (26 shorter events, 0.5 us)
Async XLA Ops:
  7.2 51.1 %copy-start = (bf16[1,2,64,2432]{3,2,1,0:T(8,128)(2,1)S(1)}, bf16[1,2,64,2432]{3,2,1,0:T(8,128)(2,1)}, u32[]{:S(2)}) copy-start(bf16[1,2,64,2432]{3,2,1,0:T(8,128)(2,1)} %param.10) | copy-start | bytes 1867780
  7.2 2.4 copy-start.3
  7.2 46.1 %all-gather.4.cloned.1.call-start = ((), (), s32[]{:S(2)}) async-start(), calls=%async_computation.2 | async-start | bytes 5603328 | tf_op jit(solution)/shard_map/all_gather | solution.py:18
  9.5 86.3 %all-gather.6.cloned.1.call-start = ((), (), s32[]{:S(2)}) async-start(), calls=%async_computation.3 | async-start | bytes 5603328 | tf_op jit(solution)/shard_map/all_gather | solution.py:19
  10.8 292.5 %all-gather.8.cloned.1.call-start = ((), (), s32[]{:S(2)}) async-start(), calls=%async_computation.4 | async-start | bytes 14786560 | tf_op jit(solution)/shard_map/all_gather | solution.py:23
  11.5 369.6 %all-reduce.3.cloned.1.call-start = ((), (), s32[]{:S(2)}) async-start(), calls=%async_computation.7 | async-start | bytes 2490368 | tf_op jit(solution)/shard_map/psum | solution.py:63
  99.6 203.7 %copy-start.2 = (bf16[1,2,64,2432]{3,2,1,0:T(8,128)(2,1)S(1)}, bf16[1,2,64,2432]{3,2,1,0:T(8,128)(2,1)}, u32[]{:S(2)}) copy-start(bf16[1,2,64,2432]{3,2,1,0:T(8,128)(2,1)} %param.11) | copy-start | bytes 1867780
  303.3 17.8 %copy-start.4 = (f32[2]{0:T(128)S(1)}, f32[2]{0:T(128)}, u32[]{:S(2)}) copy-start(f32[2]{0:T(128)} %constant.37.clone) | copy-start | bytes 28
  323.4 135.4 %reduce-scatter.9.cloned.1.call-start = ((), (), s32[]{:S(2)}) async-start(), calls=%async_computation.6 | async-start | bytes 5603328
  403.9 113.5 %reduce-scatter.7.cloned.1.call-start = ((), (), s32[]{:S(2)}) async-start(), calls=%async_computation.5 | async-start | bytes 5603328
  517.3 2.7 copy-start.1
Sparse Core Ops, SparseCore 0:
  10.5 42.7 all-gather.3
  55.7 40.0 all-gather.5
  97.4 205.8 all-gather.7
  323.5 57.5 all-reduce.2
  404.0 54.7 reduce-scatter.8
  462.2 55.1 reduce-scatter.6
where the time goes:
time: 529 us; the launch traced here: 528 us
  waiting for transfers between devices  415 us (78%)
  local copies, waits for them, and re-layouts  54.2 us (10%)
  blocking collectives  24 us (5%)
  between operations  18.8 us (4%)
  matrix products  8.36 us (2%)
  other arithmetic  7.41 us (1%)
    all_gather x1, waiting for transfers between devices, local(): lax.all_gather(frozen_weight, 'fsdp', axis=0, tiled=True)  202 us
    unnamed x8, waiting for transfers between devices  93.8 us
    psum x1, waiting for transfers between devices, local(): pairwise_down, pairwise_up = lax.psum((pairwise_down, pairwise_up), 'fsdp')  57.7 us
    unnamed x22, local copies, waits for them, and re-layouts  46 us
    all_gather x1, waiting for transfers between devices, local(): lax.all_gather(adapter_up, 'dp', axis=2, tiled=True)  37.1 us
    all_gather x1, waiting for transfers between devices, local(): lax.all_gather(adapter_down, 'dp', axis=2, tiled=True)  24.4 us
    psum x1, blocking collectives, local(): counts = lax.psum(jnp.sum(onehot, axis=0), 'dp')  15.3 us
  transfers between devices with their start and end apart: 6, of which 6 were waited for; matrix products, arithmetic and copies ran while one was open for 6% of the time, Pallas kernels for 0%

commit v1 on v0

v1 whole, which is shorter than its diff:
```python
import jax
import jax.numpy as jnp
from jax import lax
from jax.sharding import PartitionSpec as P

ADAPTER_SCALE = 0.5
BETA = 1.0
LOSS_SCALE = 64.0
F32 = jnp.float32
BF16 = jnp.bfloat16


def dot(a, b, ca, cb):
    return lax.dot_general(a, b, (((ca,), (cb,)), ((), ())), preferred_element_type=F32)


def local(latents, targets, frozen_weight, adapter_down, adapter_up, categories, timesteps):
    _, _, rows, feat = latents.shape
    classes, rank, cols = adapter_down.shape
    dp = lax.axis_size("dp")
    fs = lax.axis_size("fsdp")
    tokens = rows * fs
    cats = lax.all_gather(categories, "dp", axis=0, tiled=True)
    both = jnp.concatenate([adapter_down, adapter_up], axis=1)
    chosen = jnp.take(both, cats, axis=0)
    got = lax.all_to_all(chosen, "dp", split_axis=0, concat_axis=0, tiled=True)
    full = got.transpose(1, 0, 2).reshape(2 * rank, feat)
    down, up = full[:rank], full[rank:]
    x = latents.reshape(2 * rows, feat)
    t = targets.reshape(2 * rows, feat)
    sign = jnp.where(jnp.arange(2 * rows) < rows, 1.0, -1.0).astype(F32)[:, None]
    vz_exact = dot(up, frozen_weight, 1, 1)
    vz = vz_exact.astype(BF16)
    v = lax.all_gather(vz, "fsdp", axis=1, tiled=True)
    h = dot(x, down, 1, 1).astype(BF16)
    hs = h * sign.astype(BF16)
    g = dot(hs, x, 0, 0).astype(BF16)
    gz = lax.all_to_all(g.reshape(rank, fs, feat // fs), "fsdp", split_axis=1, concat_axis=1, tiled=True)
    gz_wide = jnp.sum(gz.astype(F32), axis=1)
    gz = gz_wide.astype(BF16)
    uu = dot(up, up, 1, 1)
    huu = ADAPTER_SCALE * lax.dot(h.astype(F32), uu, precision=lax.Precision.HIGHEST)
    s = dot(x, v, 1, 1) - dot(t, up, 1, 1) + huu
    err = jnp.sum(sign * (ADAPTER_SCALE * h.astype(F32) * (2.0 * s - huu)))
    err = err + 2.0 * ADAPTER_SCALE * jnp.sum(gz_wide * (vz_exact - vz.astype(F32)))
    diff = lax.psum(err, "fsdp") / tokens
    kappa = BETA * (0.5 + timesteps.astype(F32) / 1000.0)
    z = kappa * diff
    losses = jax.nn.softplus(z)
    total = jnp.sum((cats == categories[0]).astype(F32))
    scale = ADAPTER_SCALE * LOSS_SCALE * kappa * jax.nn.sigmoid(z) / total * 2.0 / tokens
    back = (s * sign).astype(BF16)
    pd = dot(back, x, 0, 0)
    m = dot(hs, h, 0, 0)
    pu = dot(gz, frozen_weight, 1, 0) - dot(hs, t, 0, 0) + ADAPTER_SCALE * dot(m, up.astype(F32), 1, 0)
    both = (jnp.concatenate([pd, pu], axis=0) * scale[0]).astype(BF16)
    pieces = both.reshape(2, fs, rank // fs, dp, cols).transpose(1, 3, 0, 2, 4)
    pieces = lax.all_to_all(pieces, "fsdp", split_axis=0, concat_axis=0, tiled=True)
    pieces = jnp.sum(pieces.astype(F32), axis=0).astype(BF16)
    pieces = lax.all_to_all(pieces, "dp", split_axis=0, concat_axis=0, tiled=True)
    onehot = (cats[:, None] == jnp.arange(classes, dtype=jnp.int32)[None, :]).astype(BF16)
    out = jnp.einsum("pc,pkrd->ckrd", onehot, pieces, preferred_element_type=F32).astype(BF16)
    out = lax.all_gather(out, "fsdp", axis=2, tiled=True).astype(F32)
    return out[:, 0], out[:, 1], losses


def solution(mesh):
    placed = (
        P("dp", None, "fsdp", None),
        P("dp", None, "fsdp", None),
        P("fsdp", None),
        P(None, None, "dp"),
        P(None, None, "dp"),
        P("dp"),
        P("dp"),
    )
    return jax.shard_map(
        local,
        mesh=mesh,
        in_specs=placed,
        out_specs=(P(None, None, "dp"), P(None, None, "dp"), P("dp")),
        check_vma=False,
    )
```

time: 529 us -> 167 us (0.32)
  waiting for transfers between devices: 415 us -> 19 us
  blocking collectives: 24 us -> 69.8 us
  local copies, waits for them, and re-layouts: 54.2 us -> 29.9 us
  starting transfers between devices: 0.24 us -> 15.3 us
  between operations: 18.8 us -> 6.09 us
  matrix products: 8.36 us -> 17.9 us
    all_gather x3 -> x0, waiting for transfers between devices: 264 us -> none  [the longest x1 202 us: local(): lax.all_gather(frozen_weight, 'fsdp', axis=0, tiled=True)]
    unnamed x8 -> x0, waiting for transfers between devices: 93.8 us -> none
    psum x1 -> x0, waiting for transfers between devices: 57.7 us -> none  [local(): pairwise_down, pairwise_up = lax.psum((pairwise_down, pairwise_up), 'fsdp')]
    unnamed x22 -> x12, local copies, waits for them, and re-layouts: 46 us -> 10 us
    all_gather x0 -> x2, blocking collectives: none -> 32.8 us  [the longest x1 18.1 us: local(): out = lax.all_gather(out, 'fsdp', axis=2, tiled=True).astype(F32)]
    all_to_all x0 -> x3, waiting for transfers between devices: none -> 19 us  [the longest x1 9.57 us: local(): got = lax.all_to_all(chosen, 'dp', split_axis=0, concat_axis=0, tiled=True)]
    all_to_all x0 -> x1, blocking collectives: none -> 16.2 us  [local(): lax.all_to_all(pieces, 'fsdp', split_axis=0, concat_axis=0, tiled=True)]
    all_to_all x0 -> x3, starting transfers between devices: none -> 15.3 us  [the longest x1 6.27 us: local(): lax.all_to_all(pieces, 'dp', split_axis=0, concat_axis=0, tiled=True)]
  transfers between devices with their start and end apart: 6 -> 3, of which waited for: 6 -> 3; matrix products, arithmetic and copies ran while one was open for 6% -> 3% of each run, Pallas kernels for 0% -> 0%
where the time goes in v1:
time: 167 us; the launch traced here: 166 us
  blocking collectives  69.8 us (42%)
  local copies, waits for them, and re-layouts  29.9 us (18%)
  waiting for transfers between devices  19 us (11%)
  matrix products  17.9 us (11%)
  starting transfers between devices  15.3 us (9%)
  other arithmetic  7.49 us (4%)
  between operations  6.09 us (4%)
    all_gather x1, blocking collectives, local(): out = lax.all_gather(out, 'fsdp', axis=2, tiled=True).astype(F32)  18.1 us
    dot_general x10, matrix products, dot(): lax.dot_general(a, b, (((ca,), (cb,)), ((), ())), preferred_element_type=...  17.5 us
    all_to_all x1, blocking collectives, local(): lax.all_to_all(pieces, 'fsdp', split_axis=0, concat_axis=0, tiled=True)  16.2 us
    all_gather x1, blocking collectives, local(): v = lax.all_gather(vz, 'fsdp', axis=1, tiled=True)  14.7 us
    psum x1, blocking collectives, local(): diff = lax.psum(err, 'fsdp') / tokens  11.4 us
    unnamed x12, local copies, waits for them, and re-layouts  10 us
    all_to_all x1, waiting for transfers between devices, local(): got = lax.all_to_all(chosen, 'dp', split_axis=0, concat_axis=0, tiled=True)  9.57 us
    unnamed x1, blocking collectives  9.46 us
  transfers between devices with their start and end apart: 3, of which 3 were waited for; matrix products, arithmetic and copies ran while one was open for 3% of the time, Pallas kernels for 0%

profile of v1, /device:TPU:0, one launch (start us, length us, event | category | flops | bytes accessed | tf_op | source)
XLA Modules:
  0.0 165.6 jit_solution(6114692714318431386)
XLA Ops:
  3.5 9.5 %all-reduce = s32[8]{0:T(128)S(1)} all-reduce(s32[8]{0:T(128)S(1)} %dynamic-update-slice), channel_id=1, replica_groups=mesh['dp'=8,'fsdp'=4] {'dp'}, use_global_device_ids=true, to_apply=%add | all-reduce | flops 8 | bytes 64
  13.0 2.0 %copy.37 = bf16[7,64,304]{1,2,0:T(8,128)(2,1)} copy(bf16[7,64,304]{2,1,0:T(8,128)(2,1)} %param.10) | data formatting | bytes 544768 | tf_op args[3]
  15.0 2.0 %copy.38 = bf16[7,64,304]{1,2,0:T(8,128)(2,1)} copy(bf16[7,64,304]{2,1,0:T(8,128)(2,1)} %param.11) | data formatting | bytes 544768 | tf_op args[4]
  17.0 1.5 pad_maximum_fusion
  18.6 1.5 gather_fusion
  20.0 2.0 %broadcast_select_fusion = bf16[8,128,304]{1,2,0:T(8,128)(2,1)} fusion(bf16[8,128,304]{1,2,0:T(8,128)(2,1)} %gather_fusion, pred[8]{0:T(512)(128)(4,1)S(1)} %compare_and_fusion), kind=kLoop, calls=%fused_computation.19 | loop fusion | flops 311296 | bytes 1245192 | tf_op jit(solution)/shard_map/jit(_take)/select_n | solution.py:25
  22.0 4.2 %all-to-all-start = ((bf16[8,128,304]{1,2,0:T(8,128)(2,1)}), bf16[8,128,304]{1,2,0:T(8,128)(2,1)}, u32[]{:S(2)}, u32[]{:S(2)}) async-start(bf16[8,128,304]{1,2,0:T(8,128)(2,1)} %broadcast_select_fusion), calls=%async_computation | async-start | bytes 1245184 | tf_op jit(solution)/shard_map/all_to_all | solution.py:26
  27.5 9.6 %all-to-all-done = bf16[8,128,304]{1,2,0:T(8,128)(2,1)} async-done(((bf16[8,128,304]{1,2,0:T(8,128)(2,1)}), bf16[8,128,304]{1,2,0:T(8,128)(2,1)}, u32[]{:S(2)}, u32[]{:S(2)}) %all-to-all-start) | async-done | bytes 622624 | tf_op jit(solution)/shard_map/all_to_all | solution.py:26
  37.0 2.2 %copy.39 = bf16[8,128,304]{2,1,0:T(8,128)(2,1)} copy(bf16[8,128,304]{1,2,0:T(8,128)(2,1)} %all-to-all-done) | data formatting | bytes 1245184 | tf_op jit(solution)/shard_map/all_to_all | solution.py:26
  41.5 2.1 %slice.21 = bf16[64,2432]{1,0:T(8,128)(2,1)} reshape(bf16[64,8,304]{2,1,0:T(8,128)(2,1)} %copy.42) | data formatting | bytes 622592 | tf_op jit(solution)/shard_map/slice | solution.py:28
  43.5 1.5 convolution_convert_fusion.2
  45.0 2.0 %convolution_convert_fusion = bf16[64,2432]{1,0:T(8,128)(2,1)} fusion(bf16[128,2432]{1,0:T(8,128)(2,1)} %bitcast.56, bf16[64,128]{1,0:T(8,128)(2,1)S(1)} %convolution_convert_fusion.2, bf16[128]{0:T(256)(128)(2,1)S(1)} %fusion.25), kind=kOutput, calls=%fused_computation.4 | convolution fusion | flops 40009728 | bytes 950528 | tf_op jit(solution)/shard_map/dot_general | solution.py:14
  47.1 2.1 %reshape.40 = bf16[64,4,608]{2,1,0:T(4,128)(2,1)} reshape(bf16[64,2432]{1,0:T(8,128)(2,1)} %convolution_convert_fusion) | data formatting | bytes 622592 | tf_op jit(solution)/shard_map/reshape | solution.py:38
  49.1 1.7 %copy.43 = bf16[64,4,608]{2,0,1:T(8,128)(2,1)} copy(bf16[64,4,608]{2,1,0:T(4,128)(2,1)} %reshape.40) | data formatting | bytes 622592 | tf_op jit(solution)/shard_map/reshape | solution.py:38
  50.9 4.9 %all-to-all-start.1 = ((bf16[64,4,608]{2,0,1:T(8,128)(2,1)}), bf16[64,4,608]{2,0,1:T(8,128)(2,1)}, u32[]{:S(2)}, u32[]{:S(2)}) async-start(bf16[64,4,608]{2,0,1:T(8,128)(2,1)} %copy.43), calls=%async_computation.1 | async-start | bytes 655360 | tf_op jit(solution)/shard_map/all_to_all | solution.py:38
  58.1 1.5 convolution_bitcast_fusion
  59.8 3.3 %all-to-all-done.1 = bf16[64,4,608]{2,0,1:T(8,128)(2,1)} async-done(((bf16[64,4,608]{2,0,1:T(8,128)(2,1)}), bf16[64,4,608]{2,0,1:T(8,128)(2,1)}, u32[]{:S(2)}, u32[]{:S(2)}) %all-to-all-start.1) | async-done | bytes 311328 | tf_op jit(solution)/shard_map/all_to_all | solution.py:38
  64.2 1.6 multiply_reduce_fusion
  65.8 14.7 %all-gather = bf16[4,608,64]{1,2,0:T(8,128)(2,1)S(1)} all-gather(bf16[1,608,64]{1,2,0:T(8,128)(2,1)S(1)} %get-tuple-element.23), channel_id=1, replica_groups=mesh['dp'=8,'fsdp'=4] {'fsdp'}, dimensions={0}, use_global_device_ids=true | all-gather | bytes 389120 | tf_op jit(solution)/shard_map/all_gather | solution.py:34
  81.5 2.0 %reshape.54 = bf16[2432,64]{0,1:T(8,128)(2,1)} reshape(bf16[4,608,64]{1,0,2:T(4,128)(2,1)} %copy.41) | data formatting | bytes 622592
  83.4 1.5 fusion.28
  85.0 2.0 %fusion.10 = (f32[]{:T(128)}, f32[128,64]{0,1:T(8,128)S(1)}) fusion(f32[128,64]{0,1:T(8,128)S(1)} %convolution_multiply_fusion.1, bf16[64,128]{1,0:T(8,128)(2,1)S(1)} %convolution_convert_fusion.2, f32[128]{0:T(128)S(1)} %compare_select_fusion.1, f32[64,128]{1,0:T(8,128)S(1)} %fusion.28, bf16[64,2432]{1,0:T(8,128)(2,1)S(1)} %slice.19, ...), kind=kOutput, calls=%fused_computation.28 | convolution fusion | flops 39919616 | bytes 1049092 | tf_op jit(solution)/shard_map/dot_general | solution.py:14
  88.3 1.4 fusion.7
  89.7 11.4 %psum.7 = f32[]{:T(128)} all-reduce(f32[]{:T(128)S(6)} %add.29), channel_id=1, replica_groups=mesh['dp'=8,'fsdp'=4] {'fsdp'}, use_global_device_ids=true, to_apply=%region_3.4 | all-reduce | flops 1 | bytes 8 | tf_op jit(solution)/shard_map/psum | solution.py:46
  101.8 2.3 %convolution_subtract_fusion = f32[64,2432]{1,0:T(8,128)} fusion(f32[64,2432]{1,0:T(8,128)} %fusion.7, bf16[128,2432]{1,0:T(8,128)(2,1)} %bitcast.63, bf16[64,128]{1,0:T(8,128)(2,1)S(1)} %convolution_convert_fusion.2, bf16[128]{0:T(256)(128)(2,1)S(1)} %fusion.25), kind=kOutput, calls=%fused_computation.3 | convolution fusion | flops 40009728 | bytes 1884416 | tf_op jit(solution)/shard_map/dot_general | solution.py:14
  104.1 2.3 %fusion = f32[64,2432]{1,0:T(8,128)} fusion(f32[64,2432]{1,0:T(8,128)} %convolution_subtract_fusion, bf16[64,2432]{1,0:T(8,128)(2,1)S(1)} %slice.19, bf16[64,128]{1,0:T(8,128)(2,1)S(1)} %convolution_convert_fusion.2, bf16[128]{0:T(256)(128)(2,1)S(1)} %fusion.25), kind=kOutput, calls=%fused_computation.2 | convolution fusion | flops 21291008 | bytes 1573120 | tf_op jit(solution)/shard_map/dot_general | solution.py:14
  106.4 1.4 fusion.15
  109.3 2.8 %convert_element_type.70 = bf16[2,4,16,8,304]{4,3,2,1,0:T(8,128)(2,1)} reshape(bf16[128,2432]{1,0:T(8,128)(2,1)} %fusion.1) | data formatting | bytes 1245184 | tf_op jit(solution)/shard_map/convert_element_type | solution.py:56
  113.3 16.2 %all_to_all.20 = bf16[4,8,2,16,304]{4,1,3,2,0:T(8,128)(2,1)} all-to-all(bf16[4,8,2,16,304]{4,1,3,2,0:T(8,128)(2,1)S(1)} %bitcast.59), channel_id=1, replica_groups=mesh['dp'=8,'fsdp'=4] {'fsdp'}, dimensions={0} | all-to-all | bytes 1245184 | tf_op jit(solution)/shard_map/all_to_all | solution.py:58
  131.5 6.3 %all-to-all-start.3 = ((bf16[8,2,16,304]{3,2,1,0:T(8,128)(2,1)}), bf16[8,2,16,304]{3,2,1,0:T(8,128)(2,1)S(1)}, u32[]{:S(2)}, u32[]{:S(2)}) async-start(bf16[8,2,16,304]{3,2,1,0:T(8,128)(2,1)} %copy.45), calls=%async_computation.3 | async-start | bytes 393216 | tf_op jit(solution)/shard_map/all_to_all | solution.py:60
  137.9 6.1 %all-to-all-done.3 = bf16[8,2,16,304]{3,2,1,0:T(8,128)(2,1)S(1)} async-done(((bf16[8,2,16,304]{3,2,1,0:T(8,128)(2,1)}), bf16[8,2,16,304]{3,2,1,0:T(8,128)(2,1)S(1)}, u32[]{:S(2)}, u32[]{:S(2)}) %all-to-all-start.3) | async-done | bytes 155680 | tf_op jit(solution)/shard_map/all_to_all | solution.py:60
  144.2 18.1 %all_gather.11 = bf16[7,2,64,304]{3,0,2,1:T(8,128)(2,1)S(1)} all-gather(bf16[7,2,16,304]{3,0,2,1:T(8,128)(2,1)S(1)} %convolution_convert_fusion.1), channel_id=1, replica_groups=mesh['dp'=8,'fsdp'=4] {'fsdp'}, dimensions={2}, use_global_device_ids=true | all-gather | bytes 680960 | tf_op jit(solution)/shard_map/all_gather | solution.py:63
  (29 shorter events, 15.9 us)
Async XLA Ops:
  0.6 63.6 %copy-start = (bf16[608,2432]{1,0:T(8,128)(2,1)S(1)}, bf16[608,2432]{1,0:T(8,128)(2,1)}, u32[]{:S(2)}) copy-start(bf16[608,2432]{1,0:T(8,128)(2,1)} %param.9) | copy-start | bytes 8871940
  22.0 15.0 %all-to-all-start = ((bf16[8,128,304]{1,2,0:T(8,128)(2,1)}), bf16[8,128,304]{1,2,0:T(8,128)(2,1)}, u32[]{:S(2)}, u32[]{:S(2)}) async-start(bf16[8,128,304]{1,2,0:T(8,128)(2,1)} %broadcast_select_fusion), calls=%async_computation | async-start | bytes 1245184 | tf_op jit(solution)/shard_map/all_to_all | solution.py:26
  50.9 12.3 %all-to-all-start.1 = ((bf16[64,4,608]{2,0,1:T(8,128)(2,1)}), bf16[64,4,608]{2,0,1:T(8,128)(2,1)}, u32[]{:S(2)}, u32[]{:S(2)}) async-start(bf16[64,4,608]{2,0,1:T(8,128)(2,1)} %copy.43), calls=%async_computation.1 | async-start | bytes 655360 | tf_op jit(solution)/shard_map/all_to_all | solution.py:38
  106.4 2.0 %copy-start.1 = (f32[64,2432]{1,0:T(8,128)S(1)}, f32[64,2432]{1,0:T(8,128)}, u32[]{:S(2)}) copy-start(f32[64,2432]{1,0:T(8,128)} %fusion) | copy-start | bytes 1867780
  131.5 12.5 %all-to-all-start.3 = ((bf16[8,2,16,304]{3,2,1,0:T(8,128)(2,1)}), bf16[8,2,16,304]{3,2,1,0:T(8,128)(2,1)S(1)}, u32[]{:S(2)}, u32[]{:S(2)}) async-start(bf16[8,2,16,304]{3,2,1,0:T(8,128)(2,1)} %copy.45), calls=%async_computation.3 | async-start | bytes 393216 | tf_op jit(solution)/shard_map/all_to_all | solution.py:60

commit v2 on v1

v2 whole, which is shorter than its diff:
```python
import functools

import jax
import jax.numpy as jnp
from jax import lax
from jax.experimental import pallas as pl
from jax.experimental.pallas import tpu as pltpu
from jax.sharding import PartitionSpec as P

ADAPTER_SCALE = 0.5
BETA = 1.0
LOSS_SCALE = 64.0
F32 = jnp.float32
BF16 = jnp.bfloat16
MESH = pl.DeviceIdType.MESH


def dot(a, b, cb):
    return lax.dot_general(a, b, (((1,), (cb,)), ((), ())), preferred_element_type=F32)


def halves(a):
    high = a.astype(BF16)
    return high, (a - high.astype(F32)).astype(BF16)


def kernel(dp, fs, meta, x, t, w, ad, au, gd, gu, loss,
           meta_all, us, ur, ds, dr, up, down, vr, vt, gs, gr, er, ps, pr, acc, orr,
           ms_s, ms_r, u_s, u_r, d_s, d_r, v_s, v_r, g_s, g_r, e_s, e_r, p_s, p_r, o_s, o_r):
    classes, rank, cols = ad.shape
    both_rows, feat = x.shape
    rows = both_rows // 2
    fz = feat // fs
    tokens = rows * fs
    hr = rank // 2
    rz = rank // fs
    n = dp * fs
    md, mz = lax.axis_index("dp"), lax.axis_index("fsdp")
    me = md * fs + mz

    def remote(src, dst, ss, rs, d, z):
        return pltpu.make_async_remote_copy(
            src_ref=src, dst_ref=dst, send_sem=ss, recv_sem=rs, device_id=(d, z), device_id_type=MESH)

    def each(count, body):
        def step(i, carry):
            body(i)
            return carry
        lax.fori_loop(1, count, step, 0)

    def peer_d(i):
        return lax.rem(md + i, dp)

    def peer_z(i):
        return lax.rem(mz + i, fs)

    def peer_n(i):
        lin = lax.rem(me + i, n)
        return lin // fs, lax.rem(lin, fs)

    barrier = pltpu.get_barrier_semaphore()

    def greet(i):
        d, z = peer_n(i)
        pl.semaphore_signal(barrier, inc=1, device_id=(d, z), device_id_type=MESH)

    each(n, greet)
    pl.semaphore_wait(barrier, n - 1)

    meta_all[md] = meta[...]
    each(dp, lambda i: remote(meta, meta_all.at[md], ms_s.at[i], ms_r.at[md], peer_d(i), mz).start())

    def meta_wait(i):
        d = peer_d(i)
        remote(meta, meta_all.at[d], ms_s.at[i], ms_r.at[d], d, mz).wait_recv()

    each(dp, meta_wait)

    def pick(source, d):
        cat = meta_all[d, 0:1, 0:1]
        out = jnp.zeros((rank, cols), F32)
        for c in range(classes):
            out = out + (cat == c).astype(F32) * source[c].astype(F32)
        return jnp.concatenate([out[:hr], out[hr:]], axis=1).astype(BF16)

    def send_part(source, sent, got, ss, rs):
        def body(i):
            d = peer_d(i)
            sent[d] = pick(source, d)
            remote(sent.at[d], got.at[md], ss.at[i], rs.at[md], d, mz).start()
        each(dp, body)
        got[md] = pick(source, md)

    send_part(au, us, ur, u_s, u_r)
    send_part(ad, ds, dr, d_s, d_r)

    def take_part(sent, got, ss, rs, whole):
        def body(i):
            d = peer_d(i)
            remote(sent.at[d], got.at[d], ss.at[i], rs.at[d], d, mz).wait_recv()
        each(dp, body)
        for d in range(dp):
            piece = got[d].astype(F32)
            whole[0:hr, cols * d:cols * (d + 1)] = piece[:, :cols].astype(BF16)
            whole[hr:rank, cols * d:cols * (d + 1)] = piece[:, cols:].astype(BF16)

    take_part(us, ur, u_s, u_r, up)
    v_exact = dot(up[...], w[...], 1)
    v_half = v_exact.astype(BF16)
    vr[mz] = v_half
    each(fs, lambda i: remote(vr.at[mz], vr.at[mz], v_s.at[i], v_r.at[mz], md, peer_z(i)).start())

    take_part(ds, dr, d_s, d_r, down)
    ht = dot(down[...], x[...], 1).astype(BF16)
    sign = jnp.where(lax.broadcasted_iota(jnp.int32, (1, 2 * rows), 1) < rows, 1.0, -1.0).astype(F32)
    hf = ht.astype(F32)
    hts = (hf * sign).astype(BF16)
    g = dot(hts, x[...], 0)
    for z in range(fs):
        gs[z] = g[:, fz * z:fz * (z + 1)].astype(BF16)
    each(fs, lambda i: remote(gs.at[peer_z(i)], gr.at[mz], g_s.at[i], g_r.at[mz], md, peer_z(i)).start())
    gr[mz] = gs[mz]

    uu_h, uu_l = halves(dot(up[...], up[...], 1))
    huu = ADAPTER_SCALE * (dot(uu_h, ht, 0) + dot(uu_l, ht, 0))
    st = huu - dot(up[...], t[...], 1)
    m_h, m_l = halves(ADAPTER_SCALE * dot(hts, ht, 1))
    pu = dot(m_h, up[...], 0) + dot(m_l, up[...], 0) - dot(hts, t[...], 0)

    def v_wait(i):
        z = peer_z(i)
        remote(vr.at[z], vr.at[z], v_s.at[i], v_r.at[z], md, z).wait_recv()

    each(fs, v_wait)
    for z in range(fs):
        vt[:, fz * z:fz * (z + 1)] = vr[z]
    st = st + dot(vt[...], x[...], 1)

    def g_wait(i):
        z = peer_z(i)
        remote(gs.at[z], gr.at[z], g_s.at[i], g_r.at[z], md, z).wait_recv()

    each(fs, g_wait)
    g_wide = gr[0].astype(F32)
    for z in range(1, fs):
        g_wide = g_wide + gr[z].astype(F32)
    err = jnp.sum(sign * (ADAPTER_SCALE * hf * (2.0 * st - huu)), axis=(0, 1), keepdims=True)
    err = err + 2.0 * ADAPTER_SCALE * jnp.sum(
        g_wide * (v_exact - v_half.astype(F32)), axis=(0, 1), keepdims=True)
    er[mz] = jnp.broadcast_to(err, (8, 128))
    each(fs, lambda i: remote(er.at[mz], er.at[mz], e_s.at[i], e_r.at[mz], md, peer_z(i)).start())

    back = (st * sign).astype(BF16)
    pd = dot(back, x[...], 0)
    g_h, g_l = halves(g_wide)
    pu = pu + dot(g_h, w[...], 0) + dot(g_l, w[...], 0)

    def e_wait(i):
        z = peer_z(i)
        remote(er.at[z], er.at[z], e_s.at[i], e_r.at[z], md, z).wait_recv()

    each(fs, e_wait)
    diff = er[0]
    for z in range(1, fs):
        diff = diff + er[z]
    diff = diff[0:1, :] / tokens
    my_cat = meta[0:1, :]
    kappa = BETA * (0.5 + meta[1:2, :].astype(F32) / 1000.0)
    zvalue = kappa * diff
    decay = jnp.exp(-jnp.abs(zvalue))
    loss[...] = jnp.broadcast_to(jnp.maximum(zvalue, 0.0) + jnp.log1p(decay), (8, 128))
    total = lax.fori_loop(
        0, dp, lambda d, s: s + (meta_all[d, 0:1, :] == my_cat).astype(F32), jnp.zeros((1, 128), F32))
    sigmoid = jnp.where(zvalue >= 0.0, 1.0, decay) / (1.0 + decay)
    scale = (ADAPTER_SCALE * 2.0 * LOSS_SCALE / tokens) * kappa * sigmoid / total
    pd = pd * scale[:, 0:1]
    pu = pu * scale[:, 0:1]

    for d in range(dp):
        joined = jnp.concatenate(
            [pd[:, cols * d:cols * (d + 1)], pu[:, cols * d:cols * (d + 1)]], axis=1).astype(BF16)
        for z in range(fs):
            ps[z, d] = joined[rz * z:rz * (z + 1)]

    def p_send(i):
        d, z = peer_n(i)
        remote(ps.at[z, d], pr.at[mz, md], p_s.at[z, d], p_r.at[mz, md], d, z).start()

    def p_wait(i):
        d, z = peer_n(i)
        remote(ps.at[z, d], pr.at[z, d], p_s.at[z, d], p_r.at[z, d], d, z).wait_recv()

    each(n, p_send)
    pr[mz, md] = ps[mz, md]
    acc[...] = jnp.zeros_like(acc)
    each(n, p_wait)

    def gather(d, carry):
        piece = pr[0, d].astype(F32)
        for z in range(1, fs):
            piece = piece + pr[z, d].astype(F32)
        cat = meta_all[d, 0:1, 0:1]
        for c in range(classes):
            acc[c] += (cat == c).astype(F32) * piece
        return carry

    lax.fori_loop(0, dp, gather, 0)
    orr[mz] = acc[...].astype(BF16)
    each(fs, lambda i: remote(orr.at[mz], orr.at[mz], o_s.at[i], o_r.at[mz], md, peer_z(i)).start())

    def o_wait(i):
        z = peer_z(i)
        remote(orr.at[z], orr.at[z], o_s.at[i], o_r.at[z], md, z).wait_recv()

    each(fs, o_wait)
    for z in range(fs):
        part = orr[z].astype(F32)
        gd[:, rz * z:rz * (z + 1), :] = part[:, :, :cols]
        gu[:, rz * z:rz * (z + 1), :] = part[:, :, cols:]

    def sent_d(i):
        d = peer_d(i)
        remote(meta, meta_all.at[md], ms_s.at[i], ms_r.at[md], d, mz).wait_send()
        remote(us.at[d], ur.at[md], u_s.at[i], u_r.at[md], d, mz).wait_send()
        remote(ds.at[d], dr.at[md], d_s.at[i], d_r.at[md], d, mz).wait_send()

    def sent_z(i):
        z = peer_z(i)
        remote(vr.at[mz], vr.at[mz], v_s.at[i], v_r.at[mz], md, z).wait_send()
        remote(gs.at[z], gr.at[mz], g_s.at[i], g_r.at[mz], md, z).wait_send()
        remote(er.at[mz], er.at[mz], e_s.at[i], e_r.at[mz], md, z).wait_send()
        remote(orr.at[mz], orr.at[mz], o_s.at[i], o_r.at[mz], md, z).wait_send()

    def sent_n(i):
        d, z = peer_n(i)
        remote(ps.at[z, d], pr.at[mz, md], p_s.at[z, d], p_r.at[mz, md], d, z).wait_send()

    each(dp, sent_d)
    each(fs, sent_z)
    each(n, sent_n)


def local(dp, fs, latents, targets, frozen_weight, adapter_down, adapter_up, categories, timesteps):
    _, _, rows, feat = latents.shape
    classes, rank, cols = adapter_down.shape
    fz = feat // fs
    hr, rz = rank // 2, rank // fs
    meta = jnp.concatenate([
        jnp.broadcast_to(categories[:, None], (1, 128)),
        jnp.broadcast_to(timesteps[:, None], (7, 128))], axis=0)
    vm = pl.BlockSpec(memory_space=pltpu.VMEM)
    dma = pltpu.SemaphoreType.DMA
    out = jax.ShapeDtypeStruct((classes, rank, cols), F32)
    gd, gu, loss = pl.pallas_call(
        functools.partial(kernel, dp, fs),
        out_shape=(out, out, jax.ShapeDtypeStruct((8, 128), F32)),
        in_specs=[vm] * 6,
        out_specs=(vm,) * 3,
        scratch_shapes=[
            pltpu.VMEM((dp, 8, 128), jnp.int32),
            pltpu.VMEM((dp, hr, 2 * cols), BF16),
            pltpu.VMEM((dp, hr, 2 * cols), BF16),
            pltpu.VMEM((dp, hr, 2 * cols), BF16),
            pltpu.VMEM((dp, hr, 2 * cols), BF16),
            pltpu.VMEM((rank, feat), BF16),
            pltpu.VMEM((rank, feat), BF16),
            pltpu.VMEM((fs, rank, fz), BF16),
            pltpu.VMEM((rank, feat), BF16),
            pltpu.VMEM((fs, rank, fz), BF16),
            pltpu.VMEM((fs, rank, fz), BF16),
            pltpu.VMEM((fs, 8, 128), F32),
            pltpu.VMEM((fs, dp, rz, 2 * cols), BF16),
            pltpu.VMEM((fs, dp, rz, 2 * cols), BF16),
            pltpu.VMEM((classes, rz, 2 * cols), F32),
            pltpu.VMEM((fs, classes, rz, 2 * cols), BF16),
            dma((dp,)), dma((dp,)), dma((dp,)), dma((dp,)), dma((dp,)), dma((dp,)),
            dma((fs,)), dma((fs,)), dma((fs,)), dma((fs,)), dma((fs,)), dma((fs,)),
            dma((fs, dp)), dma((fs, dp)), dma((fs,)), dma((fs,)),
        ],
        compiler_params=pltpu.CompilerParams(
            collective_id=0, has_side_effects=True, vmem_limit_bytes=48 * 1024 * 1024),
    )(meta, latents.reshape(2 * rows, feat), targets.reshape(2 * rows, feat),
      frozen_weight, adapter_down, adapter_up)
    return gd, gu, loss[0, 0:1]


def solution(mesh):
    placed = (
        P("dp", None, "fsdp", None),
        P("dp", None, "fsdp", None),
        P("fsdp", None),
        P(None, None, "dp"),
        P(None, None, "dp"),
        P("dp"),
        P("dp"),
    )
    return jax.shard_map(
        functools.partial(local, mesh.shape["dp"], mesh.shape["fsdp"]),
        mesh=mesh,
        in_specs=placed,
        out_specs=(P(None, None, "dp"), P(None, None, "dp"), P("dp")),
        check_vma=False,
    )
```

time: 167 us -> 77.5 us (0.46)
  blocking collectives: 69.8 us -> 0 us
  Pallas kernels: 0 us -> 68.4 us
  local copies, waits for them, and re-layouts: 29.9 us -> 6.39 us
  waiting for transfers between devices: 19 us -> 0 us
  matrix products: 17.9 us -> 0 us
  starting transfers between devices: 15.3 us -> 0 us
  other arithmetic: 7.49 us -> 0 us
  between operations: 6.09 us -> 1.94 us
    pallas_call x0 -> x1, Pallas kernels: none -> 68.4 us  [local(): pl.pallas_call(functools.partial(kernel, dp, fs), out_shape=(out, out, ja...]
    all_gather x2 -> x0, blocking collectives: 32.8 us -> none  [the longest x1 18.1 us: local(): out = lax.all_gather(out, 'fsdp', axis=2, tiled=True).astype(F32)]
    all_to_all x3 -> x0, waiting for transfers between devices: 19 us -> none  [the longest x1 9.57 us: local(): got = lax.all_to_all(chosen, 'dp', split_axis=0, concat_axis=0, tiled=True)]
    dot_general x12 -> x0, matrix products: 17.9 us -> none  [the longest x10 17.5 us: dot(): lax.dot_general(a, b, (((ca,), (cb,)), ((), ())), preferred_element_type=...]
    all_to_all x1 -> x0, blocking collectives: 16.2 us -> none  [local(): lax.all_to_all(pieces, 'fsdp', split_axis=0, concat_axis=0, tiled=True)]
    all_to_all x3 -> x0, starting transfers between devices: 15.3 us -> none  [the longest x1 6.27 us: local(): lax.all_to_all(pieces, 'dp', split_axis=0, concat_axis=0, tiled=True)]
    psum x1 -> x0, blocking collectives: 11.4 us -> none  [local(): diff = lax.psum(err, 'fsdp') / tokens]
    unnamed x1 -> x0, blocking collectives: 9.46 us -> none
  transfers between devices with their start and end apart: 3 -> 0, of which waited for: 3 -> 0; matrix products, arithmetic and copies ran while one was open for 3% -> 0% of each run, Pallas kernels for 0% -> 0%
where the time goes in v2:
time: 77.5 us; the launch traced here: 76.8 us
  Pallas kernels  68.4 us (88%)
  local copies, waits for them, and re-layouts  6.39 us (8%)
  between operations  1.94 us (3%)
    pallas_call x1, Pallas kernels, local(): pl.pallas_call(functools.partial(kernel, dp, fs), out_shape=(out, out, ja...  68.4 us
    unnamed x10, local copies, waits for them, and re-layouts  5.8 us

profile of v2, /device:TPU:0, one launch (start us, length us, event | category | flops | bytes accessed | tf_op | source)
XLA Modules:
  0.0 76.8 jit_solution(1622842954959176997)
XLA Ops:
  1.9 0.1 concatenate.6.meta
  2.0 0.0 copy-start
  2.0 1.1 %copy-done = bf16[1,2,64,2432]{3,2,1,0:T(8,128)(2,1)S(1)} copy-done((bf16[1,2,64,2432]{3,2,1,0:T(8,128)(2,1)S(1)}, bf16[1,2,64,2432]{3,2,1,0:T(8,128)(2,1)}, u32[]{:S(2)}) %copy-start) | copy-done | bytes 622616
  3.1 0.0 copy-start.1
  3.1 1.1 %copy-done.1 = bf16[1,2,64,2432]{3,2,1,0:T(8,128)(2,1)S(1)} copy-done((bf16[1,2,64,2432]{3,2,1,0:T(8,128)(2,1)S(1)}, bf16[1,2,64,2432]{3,2,1,0:T(8,128)(2,1)}, u32[]{:S(2)}) %copy-start.1) | copy-done | bytes 622616
  4.2 0.0 copy-start.2
  4.2 1.0 %copy-done.2 = bf16[7,64,304]{2,1,0:T(8,128)(2,1)S(1)} copy-done((bf16[7,64,304]{2,1,0:T(8,128)(2,1)S(1)}, bf16[7,64,304]{2,1,0:T(8,128)(2,1)}, u32[]{:S(2)}) %copy-start.2) | copy-done | bytes 272408
  5.1 0.0 copy-start.3
  5.1 1.0 %copy-done.3 = bf16[7,64,304]{2,1,0:T(8,128)(2,1)S(1)} copy-done((bf16[7,64,304]{2,1,0:T(8,128)(2,1)S(1)}, bf16[7,64,304]{2,1,0:T(8,128)(2,1)}, u32[]{:S(2)}) %copy-start.3) | copy-done | bytes 272408
  6.1 68.4 %shard_map.94 = (f32[7,64,304]{2,1,0:T(8,128)S(1)}, f32[7,64,304]{2,1,0:T(8,128)S(1)}, f32[8,128]{1,0:T(8,128)S(1)}) custom-call(s32[8,128]{1,0:T(8,128)S(1)} %concatenate.6.meta, bf16[128,2432]{1,0:T(8,128)(2,1)S(1)} %bitcast.5, bf16[128,2432]{1,0:T(8,128)(2,1)S(1)} %bitcast.6, bf16[608,2432]{1,0:T(8,128)(2,1)} %w.1, bf16[7,64,304]{2,1,0:T(8,128)(2,1)S(1)} %copy-done.2, ...), custom_call_target="tpu_custom_call" | custom-call | tf_op jit(solution)/shard_map/pallas_call | solution.py:254
  74.6 0.5 slice.3
  75.1 0.8 %copy.14 = f32[7,64,304]{2,1,0:T(8,128)} copy(f32[7,64,304]{2,1,0:T(8,128)S(1)} %get-tuple-element.12) | data formatting | bytes 1089536
  75.9 0.8 %copy.15 = f32[7,64,304]{2,1,0:T(8,128)} copy(f32[7,64,304]{2,1,0:T(8,128)S(1)} %get-tuple-element.13) | data formatting | bytes 1089536
  (1 shorter events, 0.0 us)
Async XLA Ops:
  2.0 1.1 %copy-start = (bf16[1,2,64,2432]{3,2,1,0:T(8,128)(2,1)S(1)}, bf16[1,2,64,2432]{3,2,1,0:T(8,128)(2,1)}, u32[]{:S(2)}) copy-start(bf16[1,2,64,2432]{3,2,1,0:T(8,128)(2,1)} %param.7) | copy-start | bytes 1867780
  3.1 1.1 %copy-start.1 = (bf16[1,2,64,2432]{3,2,1,0:T(8,128)(2,1)S(1)}, bf16[1,2,64,2432]{3,2,1,0:T(8,128)(2,1)}, u32[]{:S(2)}) copy-start(bf16[1,2,64,2432]{3,2,1,0:T(8,128)(2,1)} %param.8) | copy-start | bytes 1867780
  4.2 1.0 %copy-start.2 = (bf16[7,64,304]{2,1,0:T(8,128)(2,1)S(1)}, bf16[7,64,304]{2,1,0:T(8,128)(2,1)}, u32[]{:S(2)}) copy-start(bf16[7,64,304]{2,1,0:T(8,128)(2,1)} %ad.1) | copy-start | bytes 817156
  5.1 1.0 %copy-start.3 = (bf16[7,64,304]{2,1,0:T(8,128)(2,1)S(1)}, bf16[7,64,304]{2,1,0:T(8,128)(2,1)}, u32[]{:S(2)}) copy-start(bf16[7,64,304]{2,1,0:T(8,128)(2,1)} %au.1) | copy-start | bytes 817156

commit v3 on v2

--- a/solution.py
+++ b/solution.py
@@ -24,8 +24,8 @@
     return high, (a - high.astype(F32)).astype(BF16)
 
 
-def kernel(dp, fs, meta, x, t, w, ad, au, gd, gu, loss,
-           meta_all, us, ur, ds, dr, up, down, vr, vt, gs, gr, er, ps, pr, acc, orr,
+def kernel(dp, fs, meta, x_in, t_in, w_in, ad_in, au_in, gd, gu, loss,
+           x, t, w, ad, au, in_sem, meta_all, us, ur, ds, dr, up, down, vr, vt, gs, gr, er, ps, pr, acc, orr,
            ms_s, ms_r, u_s, u_r, d_s, d_r, v_s, v_r, g_s, g_r, e_s, e_r, p_s, p_r, o_s, o_r):
     classes, rank, cols = ad.shape
     both_rows, feat = x.shape
@@ -58,6 +58,11 @@
         lin = lax.rem(me + i, n)
         return lin // fs, lax.rem(lin, fs)
 
+    loads = [pltpu.make_async_copy(src, dst, in_sem.at[i]) for i, (src, dst) in enumerate(
+        ((au_in, au), (ad_in, ad), (w_in, w), (x_in, x), (t_in, t)))]
+    for load in loads:
+        load.start()
+
     barrier = pltpu.get_barrier_semaphore()
 
     def greet(i):
@@ -91,7 +96,9 @@
         each(dp, body)
         got[md] = pick(source, md)
 
+    loads[0].wait()
     send_part(au, us, ur, u_s, u_r)
+    loads[1].wait()
     send_part(ad, ds, dr, d_s, d_r)
 
     def take_part(sent, got, ss, rs, whole):
@@ -104,8 +111,10 @@
             whole[0:hr, cols * d:cols * (d + 1)] = piece[:, :cols].astype(BF16)
             whole[hr:rank, cols * d:cols * (d + 1)] = piece[:, cols:].astype(BF16)
 
+    for load in loads[2:]:
+        load.wait()
     take_part(us, ur, u_s, u_r, up)
-    v_exact = dot(up[...], w[...], 1)
+    v_exact = dot(w[...], up[...], 1).T
     v_half = v_exact.astype(BF16)
     vr[mz] = v_half
     each(fs, lambda i: remote(vr.at[mz], vr.at[mz], v_s.at[i], v_r.at[mz], md, peer_z(i)).start())
@@ -135,6 +144,8 @@
     for z in range(fs):
         vt[:, fz * z:fz * (z + 1)] = vr[z]
     st = st + dot(vt[...], x[...], 1)
+    back = (st * sign).astype(BF16)
+    pd = dot(back, x[...], 0)
 
     def g_wait(i):
         z = peer_z(i)
@@ -150,8 +161,6 @@
     er[mz] = jnp.broadcast_to(err, (8, 128))
     each(fs, lambda i: remote(er.at[mz], er.at[mz], e_s.at[i], e_r.at[mz], md, peer_z(i)).start())
 
-    back = (st * sign).astype(BF16)
-    pd = dot(back, x[...], 0)
     g_h, g_l = halves(g_wide)
     pu = pu + dot(g_h, w[...], 0) + dot(g_l, w[...], 0)
 
@@ -254,9 +263,15 @@
     gd, gu, loss = pl.pallas_call(
         functools.partial(kernel, dp, fs),
         out_shape=(out, out, jax.ShapeDtypeStruct((8, 128), F32)),
-        in_specs=[vm] * 6,
+        in_specs=[vm] + [pl.BlockSpec(memory_space=pl.ANY)] * 5,
         out_specs=(vm,) * 3,
         scratch_shapes=[
+            pltpu.VMEM((2 * rows, feat), BF16),
+            pltpu.VMEM((2 * rows, feat), BF16),
+            pltpu.VMEM((fz, feat), BF16),
+            pltpu.VMEM((classes, rank, cols), BF16),
+            pltpu.VMEM((classes, rank, cols), BF16),
+            dma((5,)),
             pltpu.VMEM((dp, 8, 128), jnp.int32),
             pltpu.VMEM((dp, hr, 2 * cols), BF16),
             pltpu.VMEM((dp, hr, 2 * cols), BF16),
@@ -278,7 +293,7 @@
             dma((fs, dp)), dma((fs, dp)), dma((fs,)), dma((fs,)),
         ],
         compiler_params=pltpu.CompilerParams(
-            collective_id=0, has_side_effects=True, vmem_limit_bytes=48 * 1024 * 1024),
+            collective_id=0, has_side_effects=True, vmem_limit_bytes=56 * 1024 * 1024),
     )(meta, latents.reshape(2 * rows, feat), targets.reshape(2 * rows, feat),
       frozen_weight, adapter_down, adapter_up)
     return gd, gu, loss[0, 0:1]

time: 77.5 us -> 77.4 us (level)
    unnamed x10 -> x2, local copies, waits for them, and re-layouts: 5.8 us -> 3.98 us
where the time goes in v3:
time: 77.4 us; the launch traced here: 76.8 us
  Pallas kernels  69 us (89%)
  local copies, waits for them, and re-layouts  5.84 us (8%)
  between operations  1.94 us (3%)
    pallas_call x1, Pallas kernels, local(): pl.pallas_call(functools.partial(kernel, dp, fs), out_shape=(out, out, ja...  69 us
    unnamed x2, local copies, waits for them, and re-layouts  3.98 us

profile of v3, /device:TPU:0, one launch (start us, length us, event | category | flops | bytes accessed | tf_op | source)
XLA Modules:
  0.0 76.8 jit_solution(3986139400023219576)
XLA Ops:
  1.9 0.7 concatenate.6.meta
  2.6 69.0 %shard_map.94 = (f32[7,64,304]{2,1,0:T(8,128)}, f32[7,64,304]{2,1,0:T(8,128)}, f32[8,128]{1,0:T(8,128)}) custom-call(s32[8,128]{1,0:T(8,128)} %concatenate.6.meta, bf16[128,2432]{1,0:T(8,128)(2,1)} %bitcast.5, bf16[128,2432]{1,0:T(8,128)(2,1)} %bitcast.6, bf16[608,2432]{1,0:T(8,128)(2,1)} %w_in.1, bf16[7,64,304]{2,1,0:T(8,128)(2,1)} %ad_in.1, ...), custom_call_target="tpu_custom_call" | custom-call | tf_op jit(solution)/shard_map/pallas_call | solution.py:263
  71.6 1.2 %slice.3 = f32[1,1]{1,0:T(1,128)} slice(f32[8,128]{1,0:T(8,128)} %get-tuple-element.8), slice={[0:1], [0:1]} | slice | bytes 8 | tf_op jit(solution)/shard_map/slice | solution.py:299
  72.8 2.0 %copy.14 = f32[7,64,304]{2,1,0:T(8,128)} copy(f32[7,64,304]{2,1,0:T(8,128)} %get-tuple-element.12) | data formatting | bytes 1089536
  74.8 2.0 %copy.15 = f32[7,64,304]{2,1,0:T(8,128)} copy(f32[7,64,304]{2,1,0:T(8,128)} %get-tuple-element.13) | data formatting | bytes 1089536
  (1 shorter events, 0.0 us)

commit v4 on v3

--- a/solution.py
+++ b/solution.py
@@ -25,7 +25,7 @@
 
 
 def kernel(dp, fs, meta, x_in, t_in, w_in, ad_in, au_in, gd, gu, loss,
-           x, t, w, ad, au, in_sem, meta_all, us, ur, ds, dr, up, down, vr, vt, gs, gr, er, ps, pr, acc, orr,
+           x, t, w, ad, au, in_sem, pf, meta_all, us, ur, ds, dr, up, down, vr, vt, gs, gr, er, ps, pr, acc, orr,
            ms_s, ms_r, u_s, u_r, d_s, d_r, v_s, v_r, g_s, g_r, e_s, e_r, p_s, p_r, o_s, o_r):
     classes, rank, cols = ad.shape
     both_rows, feat = x.shape
@@ -96,10 +96,11 @@
         each(dp, body)
         got[md] = pick(source, md)
 
+    loads[1].wait()
+    send_part(ad, ds, dr, d_s, d_r)
+
     loads[0].wait()
     send_part(au, us, ur, u_s, u_r)
-    loads[1].wait()
-    send_part(ad, ds, dr, d_s, d_r)
 
     def take_part(sent, got, ss, rs, whole):
         def body(i):
@@ -113,12 +114,6 @@
 
     for load in loads[2:]:
         load.wait()
-    take_part(us, ur, u_s, u_r, up)
-    v_exact = dot(w[...], up[...], 1).T
-    v_half = v_exact.astype(BF16)
-    vr[mz] = v_half
-    each(fs, lambda i: remote(vr.at[mz], vr.at[mz], v_s.at[i], v_r.at[mz], md, peer_z(i)).start())
-
     take_part(ds, dr, d_s, d_r, down)
     ht = dot(down[...], x[...], 1).astype(BF16)
     sign = jnp.where(lax.broadcasted_iota(jnp.int32, (1, 2 * rows), 1) < rows, 1.0, -1.0).astype(F32)
@@ -130,12 +125,29 @@
     each(fs, lambda i: remote(gs.at[peer_z(i)], gr.at[mz], g_s.at[i], g_r.at[mz], md, peer_z(i)).start())
     gr[mz] = gs[mz]
 
+    take_part(us, ur, u_s, u_r, up)
+    v_exact = dot(w[...], up[...], 1).T
+    v_half = v_exact.astype(BF16)
+    vr[mz] = v_half
+    each(fs, lambda i: remote(vr.at[mz], vr.at[mz], v_s.at[i], v_r.at[mz], md, peer_z(i)).start())
+
     uu_h, uu_l = halves(dot(up[...], up[...], 1))
     huu = ADAPTER_SCALE * (dot(uu_h, ht, 0) + dot(uu_l, ht, 0))
     st = huu - dot(up[...], t[...], 1)
     m_h, m_l = halves(ADAPTER_SCALE * dot(hts, ht, 1))
     pu = dot(m_h, up[...], 0) + dot(m_l, up[...], 0) - dot(hts, t[...], 0)
 
+    def g_wait(i):
+        z = peer_z(i)
+        remote(gs.at[z], gr.at[z], g_s.at[i], g_r.at[z], md, z).wait_recv()
+
+    each(fs, g_wait)
+    g_wide = gr[0].astype(F32)
+    for z in range(1, fs):
+        g_wide = g_wide + gr[z].astype(F32)
+    g_h, g_l = halves(g_wide)
+    pu = pu + dot(g_h, w[...], 0) + dot(g_l, w[...], 0)
+
     def v_wait(i):
         z = peer_z(i)
         remote(vr.at[z], vr.at[z], v_s.at[i], v_r.at[z], md, z).wait_recv()
@@ -144,25 +156,18 @@
     for z in range(fs):
         vt[:, fz * z:fz * (z + 1)] = vr[z]
     st = st + dot(vt[...], x[...], 1)
-    back = (st * sign).astype(BF16)
-    pd = dot(back, x[...], 0)
-
-    def g_wait(i):
-        z = peer_z(i)
-        remote(gs.at[z], gr.at[z], g_s.at[i], g_r.at[z], md, z).wait_recv()
-
-    each(fs, g_wait)
-    g_wide = gr[0].astype(F32)
-    for z in range(1, fs):
-        g_wide = g_wide + gr[z].astype(F32)
+
     err = jnp.sum(sign * (ADAPTER_SCALE * hf * (2.0 * st - huu)), axis=(0, 1), keepdims=True)
     err = err + 2.0 * ADAPTER_SCALE * jnp.sum(
         g_wide * (v_exact - v_half.astype(F32)), axis=(0, 1), keepdims=True)
     er[mz] = jnp.broadcast_to(err, (8, 128))
     each(fs, lambda i: remote(er.at[mz], er.at[mz], e_s.at[i], e_r.at[mz], md, peer_z(i)).start())
 
-    g_h, g_l = halves(g_wide)
-    pu = pu + dot(g_h, w[...], 0) + dot(g_l, w[...], 0)
+    back = (st * sign).astype(BF16)
+    pd = dot(back, x[...], 0)
+    for d in range(dp):
+        pf[d] = jnp.concatenate(
+            [pd[:, cols * d:cols * (d + 1)], pu[:, cols * d:cols * (d + 1)]], axis=1)
 
     def e_wait(i):
         z = peer_z(i)
@@ -182,12 +187,9 @@
         0, dp, lambda d, s: s + (meta_all[d, 0:1, :] == my_cat).astype(F32), jnp.zeros((1, 128), F32))
     sigmoid = jnp.where(zvalue >= 0.0, 1.0, decay) / (1.0 + decay)
     scale = (ADAPTER_SCALE * 2.0 * LOSS_SCALE / tokens) * kappa * sigmoid / total
-    pd = pd * scale[:, 0:1]
-    pu = pu * scale[:, 0:1]
 
     for d in range(dp):
-        joined = jnp.concatenate(
-            [pd[:, cols * d:cols * (d + 1)], pu[:, cols * d:cols * (d + 1)]], axis=1).astype(BF16)
+        joined = (pf[d] * scale[:, 0:1]).astype(BF16)
         for z in range(fs):
             ps[z, d] = joined[rz * z:rz * (z + 1)]
 
@@ -272,6 +274,7 @@
             pltpu.VMEM((classes, rank, cols), BF16),
             pltpu.VMEM((classes, rank, cols), BF16),
             dma((5,)),
+            pltpu.VMEM((dp, rank, 2 * cols), F32),
             pltpu.VMEM((dp, 8, 128), jnp.int32),
             pltpu.VMEM((dp, hr, 2 * cols), BF16),
             pltpu.VMEM((dp, hr, 2 * cols), BF16),

time: 77.4 us -> 76.8 us (level)
  no operation moved by 1% of the time
where the time goes in v4:
time: 76.8 us; the launch traced here: 76.2 us
  Pallas kernels  68.4 us (89%)
  local copies, waits for them, and re-layouts  5.84 us (8%)
  between operations  1.94 us (3%)
    pallas_call x1, Pallas kernels, local(): pl.pallas_call(functools.partial(kernel, dp, fs), out_shape=(out, out, ja...  68.4 us
    unnamed x2, local copies, waits for them, and re-layouts  3.98 us

profile of v4, /device:TPU:0, one launch (start us, length us, event | category | flops | bytes accessed | tf_op | source)
XLA Modules:
  0.0 76.2 jit_solution(12915407506643184326)
XLA Ops:
  1.9 0.7 concatenate.6.meta
  2.6 68.4 %shard_map.94 = (f32[7,64,304]{2,1,0:T(8,128)}, f32[7,64,304]{2,1,0:T(8,128)}, f32[8,128]{1,0:T(8,128)}) custom-call(s32[8,128]{1,0:T(8,128)} %concatenate.6.meta, bf16[128,2432]{1,0:T(8,128)(2,1)} %bitcast.5, bf16[128,2432]{1,0:T(8,128)(2,1)} %bitcast.6, bf16[608,2432]{1,0:T(8,128)(2,1)} %w_in.1, bf16[7,64,304]{2,1,0:T(8,128)(2,1)} %ad_in.1, ...), custom_call_target="tpu_custom_call" | custom-call | tf_op jit(solution)/shard_map/pallas_call | solution.py:265
  71.0 1.2 %slice.3 = f32[1,1]{1,0:T(1,128)} slice(f32[8,128]{1,0:T(8,128)} %get-tuple-element.8), slice={[0:1], [0:1]} | slice | bytes 8 | tf_op jit(solution)/shard_map/slice | solution.py:302
  72.2 2.0 %copy.14 = f32[7,64,304]{2,1,0:T(8,128)} copy(f32[7,64,304]{2,1,0:T(8,128)} %get-tuple-element.12) | data formatting | bytes 1089536
  74.2 2.0 %copy.15 = f32[7,64,304]{2,1,0:T(8,128)} copy(f32[7,64,304]{2,1,0:T(8,128)} %get-tuple-element.13) | data formatting | bytes 1089536
  (1 shorter events, 0.0 us)

commit v5 on v4

--- a/solution.py
+++ b/solution.py
@@ -197,14 +197,12 @@
         d, z = peer_n(i)
         remote(ps.at[z, d], pr.at[mz, md], p_s.at[z, d], p_r.at[mz, md], d, z).start()
 
-    def p_wait(i):
-        d, z = peer_n(i)
+    def p_wait(d, z):
         remote(ps.at[z, d], pr.at[z, d], p_s.at[z, d], p_r.at[z, d], d, z).wait_recv()
 
     each(n, p_send)
     pr[mz, md] = ps[mz, md]
     acc[...] = jnp.zeros_like(acc)
-    each(n, p_wait)
 
     def gather(d, carry):
         piece = pr[0, d].astype(F32)
@@ -215,7 +213,16 @@
             acc[c] += (cat == c).astype(F32) * piece
         return carry
 
-    lax.fori_loop(0, dp, gather, 0)
+    each(fs, lambda i: p_wait(md, peer_z(i)))
+    gather(md, 0)
+
+    def p_take(i):
+        d = lax.rem(md + dp - i, dp)
+        for z in range(fs):
+            p_wait(d, z)
+        gather(d, 0)
+
+    each(dp, p_take)
     orr[mz] = acc[...].astype(BF16)
     each(fs, lambda i: remote(orr.at[mz], orr.at[mz], o_s.at[i], o_r.at[mz], md, peer_z(i)).start())
 

time: 76.8 us -> 76.2 us (level)
  no operation moved by 1% of the time
where the time goes in v5:
time: 76.2 us; the launch traced here: 75.7 us
  Pallas kernels  67.9 us (89%)
  local copies, waits for them, and re-layouts  5.84 us (8%)
  between operations  1.94 us (3%)
    pallas_call x1, Pallas kernels, local(): pl.pallas_call(functools.partial(kernel, dp, fs), out_shape=(out, out, ja...  67.9 us
    unnamed x2, local copies, waits for them, and re-layouts  3.98 us

profile of v5, /device:TPU:0, one launch (start us, length us, event | category | flops | bytes accessed | tf_op | source)
XLA Modules:
  0.0 75.7 jit_solution(14513934546499405155)
XLA Ops:
  1.9 0.7 concatenate.6.meta
  2.6 67.9 %shard_map.94 = (f32[7,64,304]{2,1,0:T(8,128)}, f32[7,64,304]{2,1,0:T(8,128)}, f32[8,128]{1,0:T(8,128)}) custom-call(s32[8,128]{1,0:T(8,128)} %concatenate.6.meta, bf16[128,2432]{1,0:T(8,128)(2,1)} %bitcast.5, bf16[128,2432]{1,0:T(8,128)(2,1)} %bitcast.6, bf16[608,2432]{1,0:T(8,128)(2,1)} %w_in.1, bf16[7,64,304]{2,1,0:T(8,128)(2,1)} %ad_in.1, ...), custom_call_target="tpu_custom_call" | custom-call | tf_op jit(solution)/shard_map/pallas_call | solution.py:272
  70.5 1.2 %slice.3 = f32[1,1]{1,0:T(1,128)} slice(f32[8,128]{1,0:T(8,128)} %get-tuple-element.8), slice={[0:1], [0:1]} | slice | bytes 8 | tf_op jit(solution)/shard_map/slice | solution.py:309
  71.7 2.0 %copy.14 = f32[7,64,304]{2,1,0:T(8,128)} copy(f32[7,64,304]{2,1,0:T(8,128)} %get-tuple-element.12) | data formatting | bytes 1089536
  73.7 2.0 %copy.15 = f32[7,64,304]{2,1,0:T(8,128)} copy(f32[7,64,304]{2,1,0:T(8,128)} %get-tuple-element.13) | data formatting | bytes 1089536
  (1 shorter events, 0.0 us)
